TPU v7x, 512 devices: a whole 4x4x16 slice. The times are simulated.
512 devices in a mesh: row: 16 (over y, z_lo), col: 32 (over z_hi, x, core).
Axes of the slice: x: 4, y: 4, z: 16 (z_hi: 4, z_lo: 4; z = z_hi * 4 + z_lo), core: 2. Of those that a mesh axis runs over, the one named last changes fastest.
Arguments:
- grid: bfloat16 [512, 1024, 256], P('row', 'col'), may hold values from -6 to 6
- row_gain: float32 [256], replicated, may hold values from 0.1 to 1.9
- row_qkv: bfloat16 [256, 768], replicated, may hold values from -24 to 24, as said below
- row_out: bfloat16 [256, 256], replicated, may hold values from -1.5 to 1.5
- col_gain: float32 [256], replicated, may hold values from 0.1 to 1.9
- col_qkv: bfloat16 [256, 768], replicated, may hold values from -24 to 24, as said below
- col_out: bfloat16 [256, 256], replicated, may hold values from -1.5 to 1.5
Outputs:
- updated: bfloat16 [512, 1024, 256], P('row', 'col')
Inputs may be any that keep to these rules, and one draw needn't show every extreme that they name: `row_qkv`: projection weights of fan-in 256. `col_qkv`: projection weights of fan-in 256.
All inputs are finite; a program needn't handle non-finite values.
Results may differ from a plain program's by a relative error of at most 0.028.
Values may be sent and summed in bfloat16 or wider, within the bound.
No kernel may reach another device: no remote copies, remote signals or barrier semaphores. Data moves between devices by JAX's collectives and lax.ppermute only.
A program may use at most 64 MiB of HBM per device.

v0:
```python
import jax
import jax.numpy as jnp
from jax import lax
from jax.sharding import PartitionSpec as P

HEADS = 8


def layer_norm(values, gain):
    as_float = values.astype(jnp.float32)
    mean_val = jnp.mean(as_float, axis=-1, keepdims=True)
    centred = as_float - mean_val
    variance = jnp.mean(centred * centred, axis=-1, keepdims=True)
    return (centred * lax.rsqrt(variance + 1e-05) * gain).astype(jnp.bfloat16)


def project_cells(items, weight):
    leading = items.shape[:-1]
    flattened = items.reshape(-1, items.shape[-1])
    result = jnp.dot(flattened, weight, preferred_element_type=jnp.float32).astype(jnp.bfloat16)
    return result.reshape(leading + (weight.shape[1],))


def heads_attend(packed):
    lines_count, length, triple = packed.shape
    channels = triple // 3
    head_dim = channels // HEADS
    stacked = packed.reshape(lines_count, length, 3, HEADS, head_dim).transpose(2, 3, 0, 1, 4)

    def single_head(triplet):
        queries, keys, values = triplet
        scores = jnp.einsum(
            "nld,nmd->nlm", queries, keys, preferred_element_type=jnp.float32
        ) * head_dim ** (-0.5)
        peak = jnp.max(scores, axis=-1, keepdims=True)
        exponent = jnp.exp(scores - peak)
        shares = (exponent / jnp.sum(exponent, axis=-1, keepdims=True)).astype(jnp.bfloat16)
        return jnp.einsum("nlm,nmd->nld", shares, values, preferred_element_type=jnp.float32)

    per_head = lax.map(single_head, (stacked[0], stacked[1], stacked[2]))
    return (
        per_head.transpose(1, 2, 0, 3).reshape(lines_count, length, channels).astype(jnp.bfloat16)
    )


def row_items(items):
    return heads_attend(items[0])[None]


def col_items(items):
    result = heads_attend(items[:, 0].transpose(1, 0, 2))
    return result.transpose(1, 0, 2)[:, None]


def add_output(base, attended, weight):
    width = base.shape[-1]
    projected = jnp.dot(attended.reshape(-1, width), weight, preferred_element_type=jnp.float32)
    return (base.astype(jnp.float32) + projected.reshape(base.shape)).astype(jnp.bfloat16)


def on_device(grid, row_gain, row_qkv, row_out, col_gain, col_qkv, col_out):
    rows_blk, cols_blk, width = grid.shape
    col_count = lax.axis_size("col")
    row_count = lax.axis_size("row")
    normed = layer_norm(grid, row_gain)
    grouped = normed.reshape(col_count, rows_blk // col_count, cols_blk, width)
    packed = project_cells(grouped, row_qkv)
    row_lines = row_items(lax.all_to_all(packed, "col", split_axis=0, concat_axis=2, tiled=True))
    returned = lax.all_to_all(row_lines, "col", split_axis=2, concat_axis=0, tiled=True).reshape(
        rows_blk, cols_blk, width
    )
    middle = add_output(grid, returned, row_out)
    normed_col = layer_norm(middle, col_gain).reshape(
        rows_blk, row_count, cols_blk // row_count, width
    )
    packed_col = project_cells(normed_col, col_qkv)
    col_lines = col_items(
        lax.all_to_all(packed_col, "row", split_axis=1, concat_axis=0, tiled=True)
    )
    returned_col = lax.all_to_all(
        col_lines, "row", split_axis=0, concat_axis=1, tiled=True
    ).reshape(rows_blk, cols_blk, width)
    return add_output(middle, returned_col, col_out)


def solution(mesh):
    in_specs = (P("row", "col", None), P(), P(), P(), P(), P(), P())
    out_specs = P("row", "col", None)
    return jax.shard_map(
        on_device, mesh=mesh, in_specs=in_specs, out_specs=out_specs, check_vma=False
    )
```

profile of v0, /device:TPU:1, one launch (start us, length us, event | category | flops | bytes accessed | tf_op | source)
XLA Modules:
  0.0 305.1 jit_solution(10676893359948665993)
XLA Ops:
  0.0 1.3 convert_reduce_fusion.1
  1.3 1.4 fusion.68
  2.8 1.4 fusion.70
  4.2 1.7 convolution_convert_fusion.1
  5.9 19.2 %all-to-all-start = ((bf16[32,1,32,768]{3,2,1,0:T(8,128)(2,1)}), bf16[32,1,32,768]{3,2,1,0:T(8,128)(2,1)S(1)}, u32[]{:S(2)}, u32[]{:S(2)}) async-start(bf16[32,1,32,768]{3,2,1,0:T(8,128)(2,1)} %bitcast.10), calls=%async_computation | async-start | bytes 3145728 | tf_op jit(solution)/shard_map/all_to_all | solution.py:68
  25.1 75.1 %all-to-all-done = bf16[32,1,32,768]{3,2,1,0:T(8,128)(2,1)S(1)} async-done(((bf16[32,1,32,768]{3,2,1,0:T(8,128)(2,1)}), bf16[32,1,32,768]{3,2,1,0:T(8,128)(2,1)S(1)}, u32[]{:S(2)}, u32[]{:S(2)}) %all-to-all-start) | async-done | bytes 1572896 | tf_op jit(solution)/shard_map/all_to_all | solution.py:68
  100.3 5.5 %reshape_squeeze.3 = bf16[1,1024,3,8,32]{4,3,2,1,0:T(8,128)(2,1)} reshape(bf16[32,1,32,768]{3,2,1,0:T(8,128)(2,1)S(1)} %all-to-all-done) | data formatting | bytes 3145728 | tf_op jit(solution)/shard_map/reshape;squeeze | solution.py:28
  105.8 3.3 %slice_bitcast_fusion = (bf16[8,1,1024,32]{3,0,2,1:T(8,128)(2,1)S(1)}, bf16[8,1,1024,32]{3,0,2,1:T(8,128)(2,1)S(1)}, bf16[8,1,1024,32]{3,0,2,1:T(8,128)(2,1)S(1)}) fusion(bf16[3,8,1,1024,32]{4,1,0,3,2:T(8,128)(2,1)} %bitcast.143), kind=kLoop, calls=%fused_computation.43 | loop fusion | bytes 3145728 | tf_op jit(solution)/shard_map/squeeze | solution.py:40
  109.3 1.7 copy.42
  111.0 1.6 copy.43
  112.6 34.7 %while.20 = (s32[]{:T(128)}, bf16[8,1,1024,32]{2,3,1,0:T(8,128)(2,1)S(1)}, bf16[8,1,1024,32]{3,2,1,0:T(8,128)(2,1)S(1)}, bf16[8,1,1024,32]{3,2,1,0:T(8,128)(2,1)}, bf16[8,1,1024,32]{3,2,1,0:T(8,128)(2,1)}, /*index=5*/s32[]{:T(128)}) while((s32[]{:T(128)}, bf16[8,1,1024,32]{2,3,1,0:T(8,128)(2,1)S(1)}, bf16[8,1,1024,32]{3,2,1,0:T(8,128)(2,1)S(1)}, ...), condition=%wide.region_5.6_spmd, body=%wide.region_2.5_spmd.sunk | while | flops 143652864 | bytes 13523013 | solution.py:40
  112.6 1.7 multiply_reduce_fusion.3
  114.3 0.7 fusion.96
  115.0 1.9 fusion.97
  117.0 1.7 multiply_reduce_fusion.3
  118.6 0.7 fusion.96
  119.4 1.9 fusion.97
  121.3 1.7 multiply_reduce_fusion.3
  123.0 0.7 fusion.96
  123.7 1.9 fusion.97
  125.6 1.7 multiply_reduce_fusion.3
  127.3 0.7 fusion.96
  128.0 1.9 fusion.97
  130.0 1.7 multiply_reduce_fusion.3
  131.6 0.7 fusion.96
  132.4 1.9 fusion.97
  134.3 1.7 multiply_reduce_fusion.3
  136.0 0.7 fusion.96
  136.7 1.9 fusion.97
  138.6 1.7 multiply_reduce_fusion.3
  140.3 0.7 fusion.96
  141.1 1.9 fusion.97
  143.0 1.7 multiply_reduce_fusion.3
  144.7 0.7 fusion.96
  145.4 1.9 fusion.97
  147.3 0.9 copy.45
  148.7 3.8 %reduce.4 = bf16[1024,256]{1,0:T(8,128)(2,1)S(1)} reduce(bf16[1024,1,1,256]{3,2,1,0:T(2,128)(2,1)S(1)} %bitcast.147, bf16[]{:T(256)} %broadcast.84), dimensions={1,2}, to_apply=%bitcast.105.reduce_sub_computation | reduce | bytes 1048578
  152.7 37.4 %all_to_all.48 = bf16[32,2,4096]{2,1,0:T(2,128)(2,1)S(1)} all-to-all(bf16[32,2,4096]{2,1,0:T(2,128)(2,1)S(1)} %reshape.107), channel_id=1, replica_groups=mesh['row'=16,'col'=32] {'col'}, dimensions={0} | all-to-all | bytes 1048576 | tf_op jit(solution)/shard_map/all_to_all | solution.py:69
  192.5 1.5 reshape.103
  194.0 3.4 %copy.46 = bf16[32,16,2,768]{3,0,2,1:T(8,128)(2,1)} copy(bf16[32,16,2,768]{3,2,1,0:T(2,128)(2,1)} %reshape.103) | data formatting | bytes 3145728 | tf_op jit(solution)/shard_map/reshape | solution.py:21
  197.4 10.1 %all-to-all-start.2 = ((bf16[32,16,2,768]{3,0,2,1:T(8,128)(2,1)}), bf16[32,16,2,768]{3,0,2,1:T(8,128)(2,1)S(1)}, u32[]{:S(2)}, u32[]{:S(2)}) async-start(bf16[32,16,2,768]{3,0,2,1:T(8,128)(2,1)} %copy.46), calls=%async_computation.2 | async-start | bytes 3145728 | tf_op jit(solution)/shard_map/all_to_all | solution.py:78
  207.6 42.7 %all-to-all-done.2 = bf16[32,16,2,768]{3,0,2,1:T(8,128)(2,1)S(1)} async-done(((bf16[32,16,2,768]{3,0,2,1:T(8,128)(2,1)}), bf16[32,16,2,768]{3,0,2,1:T(8,128)(2,1)S(1)}, u32[]{:S(2)}, u32[]{:S(2)}) %all-to-all-start.2) | async-done | bytes 1572896 | tf_op jit(solution)/shard_map/all_to_all | solution.py:78
  250.3 1.3 copy.47
  251.5 1.7 copy.48
  253.3 1.1 slice_bitcast_fusion.3
  254.4 29.6 %while.21 = (s32[]{:T(128)}, bf16[8,2,512,32]{2,3,0,1:T(8,128)(2,1)S(1)}, bf16[8,2,512,32]{2,3,0,1:T(8,128)(2,1)}, bf16[8,2,512,32]{2,3,0,1:T(8,128)(2,1)}, bf16[8,2,512,32]{2,3,0,1:T(8,128)(2,1)S(1)}, /*index=5*/s32[]{:T(128)}) while((s32[]{:T(128)}, bf16[8,2,512,32]{2,3,0,1:T(8,128)(2,1)S(1)}, bf16[8,2,512,32]{2,3,0,1:T(8,128)(2,1)}, ...), condition=%wide.region_11.12_spmd, body=%wide.region_8.11_spmd.sunk | while | flops 104335360 | bytes 470085 | solution.py:40
  254.4 1.7 fusion.104
  256.1 2.0 fusion.105
  258.0 1.7 fusion.104
  259.8 2.0 fusion.105
  261.8 1.7 fusion.104
  263.5 2.0 fusion.105
  265.5 1.7 fusion.104
  267.2 2.0 fusion.105
  269.2 1.7 fusion.104
  270.9 2.0 fusion.105
  272.9 1.7 fusion.104
  274.6 2.0 fusion.105
  276.6 1.7 fusion.104
  278.3 2.0 fusion.105
  280.3 1.7 fusion.104
  282.0 2.0 fusion.105
  284.5 18.7 %all_to_all.49 = bf16[512,1,2,256]{3,2,1,0:T(2,128)(2,1)S(1)} all-to-all(bf16[512,1,2,256]{3,2,1,0:T(2,128)(2,1)S(1)} %copy.53), channel_id=1, replica_groups=mesh['row'=16,'col'=32] {'row'}, dimensions={0} | all-to-all | bytes 1048576 | tf_op jit(solution)/shard_map/all_to_all | solution.py:80
  304.0 1.1 fusion.60
  (31 shorter events, 4.5 us)
Async XLA Ops:
  0.0 4.2 %copy-start = (bf16[256,768]{1,0:T(8,128)(2,1)S(1)}, bf16[256,768]{1,0:T(8,128)(2,1)}, u32[]{:S(2)}) copy-start(bf16[256,768]{1,0:T(8,128)(2,1)} %param.13) | copy-start | bytes 1179652
  5.9 94.4 %all-to-all-start = ((bf16[32,1,32,768]{3,2,1,0:T(8,128)(2,1)}), bf16[32,1,32,768]{3,2,1,0:T(8,128)(2,1)S(1)}, u32[]{:S(2)}, u32[]{:S(2)}) async-start(bf16[32,1,32,768]{3,2,1,0:T(8,128)(2,1)} %bitcast.10), calls=%async_computation | async-start | bytes 3145728 | tf_op jit(solution)/shard_map/all_to_all | solution.py:68
  152.7 38.1 %copy-start.1 = (bf16[32,32,256]{2,1,0:T(8,128)(2,1)S(1)}, bf16[32,32,256]{2,1,0:T(8,128)(2,1)}, u32[]{:S(2)}) copy-start(bf16[32,32,256]{2,1,0:T(8,128)(2,1)} %param.11) | copy-start | bytes 1572868
  152.7 38.1 %copy-start.3 = (bf16[256,256]{1,0:T(8,128)(2,1)S(1)}, bf16[256,256]{1,0:T(8,128)(2,1)}, u32[]{:S(2)}) copy-start(bf16[256,256]{1,0:T(8,128)(2,1)} %param.14) | copy-start | bytes 393220
  190.6 0.9 copy-start.5
  190.7 1.2 copy-start.2
  197.4 52.8 %all-to-all-start.2 = ((bf16[32,16,2,768]{3,0,2,1:T(8,128)(2,1)}), bf16[32,16,2,768]{3,0,2,1:T(8,128)(2,1)S(1)}, u32[]{:S(2)}, u32[]{:S(2)}) async-start(bf16[32,16,2,768]{3,0,2,1:T(8,128)(2,1)} %copy.46), calls=%async_computation.2 | async-start | bytes 3145728 | tf_op jit(solution)/shard_map/all_to_all | solution.py:78
  284.5 19.5 %copy-start.4 = (bf16[256,256]{1,0:T(8,128)(2,1)S(1)}, bf16[256,256]{1,0:T(8,128)(2,1)}, u32[]{:S(2)}) copy-start(bf16[256,256]{1,0:T(8,128)(2,1)} %param.17) | copy-start | bytes 393220
where the time goes:
time: 307 us; the launch traced here: 305 us
  waiting for transfers between devices  118 us (38%)
  matrix products  62 us (20%)
  blocking collectives  56.1 us (18%)
  starting transfers between devices  29.3 us (10%)
  local copies, waits for them, and re-layouts  24.8 us (8%)
  other arithmetic  14.5 us (5%)
    all_to_all x1, waiting for transfers between devices, on_device(): lax.all_to_all(packed, 'col', split_axis=0, concat_axis=2, tiled=True)  75.1 us
    all_to_all x1, waiting for transfers between devices, on_device(): lax.all_to_all(packed_col, 'row', split_axis=1, concat_axis=0, tiled=True)  42.7 us
    all_to_all x1, blocking collectives, on_device(): lax.all_to_all(row_lines, 'col', split_axis=2, concat_axis=0, tiled=True)  37.4 us
    dot_general x16, matrix products, single_head(): jnp.einsum('nlm,nmd->nld', shares, values, preferred_element_type=jnp.flo...  31.1 us
    all_to_all x1, starting transfers between devices, on_device(): lax.all_to_all(packed, 'col', split_axis=0, concat_axis=2, tiled=True)  19.2 us
    all_to_all x1, blocking collectives, on_device(): lax.all_to_all(col_lines, 'row', split_axis=0, concat_axis=1, tiled=True)  18.7 us
    sub x8, matrix products, single_head(): exponent = jnp.exp(scores - peak)  13.8 us
    dot_general x8, matrix products, single_head(): jnp.einsum('nld,nmd->nlm', queries, keys, preferred_element_type=jnp.floa...  13.4 us
  transfers between devices with their start and end apart: 2, of which 2 were waited for; matrix products, arithmetic and copies ran while one was open for 0% of the time, Pallas kernels for 0%

commit v1 on v0

v1 whole, which is shorter than its diff:
```python
import functools
import math

import jax
import jax.numpy as jnp
from jax import lax
from jax.experimental import pallas as pl
from jax.experimental.pallas import tpu as pltpu
from jax.sharding import PartitionSpec as P

HEADS = 8
QUERY_BLOCK = 256
EPS = 1e-05


def contract(a, b, dim_a, dim_b):
    dims = (((dim_a,), (dim_b,)), ((), ()))
    return lax.dot_general(a, b, dims, preferred_element_type=jnp.float32)


def layer_norm(values, gain):
    centred = values - jnp.mean(values, axis=-1, keepdims=True)
    variance = jnp.mean(centred * centred, axis=-1, keepdims=True)
    return (centred * lax.rsqrt(variance + EPS) * gain).astype(jnp.bfloat16)


def lines_kernel(cells_ref, gain_ref, qkv_ref, out_ref, result_ref, q_ref, kt_ref, v_ref, att_ref, *, lines):
    cells, width = cells_ref.shape
    length = cells // lines
    head_dim = width // HEADS
    scale = head_dim**-0.5 * math.log2(math.e)
    normed = layer_norm(cells_ref[...].astype(jnp.float32), gain_ref[...])
    q_ref[...] = (contract(normed, qkv_ref[:, :width], 1, 0) * scale).astype(jnp.bfloat16)
    kt_ref[...] = contract(qkv_ref[:, width : 2 * width], normed, 0, 1).astype(jnp.bfloat16)
    v_ref[...] = contract(normed, qkv_ref[:, 2 * width :], 1, 0).astype(jnp.bfloat16)
    block = min(QUERY_BLOCK, length)
    head_of_v = lax.broadcasted_iota(jnp.int32, (length, width), 1) // head_dim
    head_of_q = lax.broadcasted_iota(jnp.int32, (block, width), 1) // head_dim
    zero, one = jnp.zeros((), jnp.bfloat16), jnp.ones((), jnp.bfloat16)
    for line in range(lines):
        keys = slice(line * length, (line + 1) * length)
        for start in range(line * length, (line + 1) * length, block):
            rows = slice(start, start + block)
            attended = jnp.zeros((block, width), jnp.float32)
            for head in range(HEADS):
                queries = jnp.where(head_of_q == head, q_ref[rows, :], zero)
                scores = contract(queries, kt_ref[:, keys], 1, 0)
                peak = jnp.max(scores, axis=1, keepdims=True)
                shares = jnp.exp2(scores - peak).astype(jnp.bfloat16)
                values = jnp.where(head_of_v == head, v_ref[keys, :], one)
                total = contract(shares, values, 1, 0)
                half = width // 2
                sums = jnp.concatenate([total[:, half:], total[:, :half]], axis=1)
                attended = jnp.where(head_of_q == head, total / sums, attended)
            att_ref[rows, :] = attended.astype(jnp.bfloat16)
    added = contract(att_ref[...], out_ref[...], 1, 0)
    result_ref[...] = (cells_ref[...].astype(jnp.float32) + added).astype(jnp.bfloat16)


def attend(cells, gain, qkv, out, lines):
    count, width = cells.shape
    whole = pl.BlockSpec(memory_space=pltpu.VMEM)
    return pl.pallas_call(
        functools.partial(lines_kernel, lines=lines),
        out_shape=jax.ShapeDtypeStruct((count, width), jnp.bfloat16),
        in_specs=[whole] * 4,
        out_specs=whole,
        scratch_shapes=[
            pltpu.VMEM((count, width), jnp.bfloat16),
            pltpu.VMEM((width, count), jnp.bfloat16),
            pltpu.VMEM((count, width), jnp.bfloat16),
            pltpu.VMEM((count, width), jnp.bfloat16),
        ],
        compiler_params=pltpu.CompilerParams(vmem_limit_bytes=40 << 20),
        name=f"attend_{lines}_lines",
    )(cells, gain.reshape(1, width), qkv, out)


def on_device(grid, row_gain, row_qkv, row_out, col_gain, col_qkv, col_out):
    rows_blk, cols_blk, width = grid.shape
    col_count = lax.axis_size("col")
    row_count = lax.axis_size("row")
    pair = cols_blk // row_count
    cells = lax.all_to_all(grid, "col", split_axis=0, concat_axis=0, tiled=True)
    middle = attend(cells.reshape(-1, width), row_gain, row_qkv, row_out, 1)
    to_cols = middle.reshape(col_count, pair, row_count, width).transpose(0, 2, 1, 3)
    to_cols = to_cols.reshape(col_count * row_count, pair, width)
    col_cells = lax.all_to_all(to_cols, ("col", "row"), split_axis=0, concat_axis=0, tiled=True)
    lines = col_cells.transpose(1, 0, 2).reshape(-1, width)
    updated = attend(lines, col_gain, col_qkv, col_out, pair)
    back = updated.reshape(pair, col_count, row_count, width).transpose(2, 1, 0, 3)
    home = lax.all_to_all(back, "row", split_axis=0, concat_axis=0, tiled=True)
    return home.transpose(1, 2, 0, 3).reshape(rows_blk, cols_blk, width)


def solution(mesh):
    in_specs = (P("row", "col", None), P(), P(), P(), P(), P(), P())
    out_specs = P("row", "col", None)
    return jax.shard_map(
        on_device, mesh=mesh, in_specs=in_specs, out_specs=out_specs, check_vma=False
    )
```

time: 307 us -> 139 us (0.45)
  waiting for transfers between devices: 118 us -> 0 us
  matrix products: 62 us -> 0 us
  blocking collectives: 56.1 us -> 118 us
  starting transfers between devices: 29.3 us -> 0 us
  local copies, waits for them, and re-layouts: 24.8 us -> 3.45 us
  Pallas kernels: 0 us -> 16.7 us
  other arithmetic: 14.5 us -> 0 us
    all_to_all x2 -> x0, waiting for transfers between devices: 118 us -> none  [the longest x1 75.1 us: on_device(): lax.all_to_all(packed, 'col', split_axis=0, concat_axis=2, tiled=True)]
    all_to_all x2 -> x3, blocking collectives: 56.1 us -> 118 us  [the longest x1 49.4 us: on_device(): lax.all_to_all(to_cols, ('col', 'row'), split_axis=0, concat_axis=0, tile...]
    dot_general x28 -> x0, matrix products: 48.2 us -> none  [the longest x16 31.1 us: single_head(): jnp.einsum('nlm,nmd->nld', shares, values, preferred_element_type=jnp.flo...]
    all_to_all x2 -> x0, starting transfers between devices: 29.3 us -> none  [the longest x1 19.2 us: on_device(): lax.all_to_all(packed, 'col', split_axis=0, concat_axis=2, tiled=True)]
    pallas_call x0 -> x2, Pallas kernels: none -> 16.7 us  [attend(): pl.pallas_call(functools.partial(lines_kernel, lines=lines), out_shape=ja...]
    sub x8 -> x0, matrix products: 13.8 us -> none  [single_head(): exponent = jnp.exp(scores - peak)]
    reduce_sum x11 -> x0, other arithmetic: 8.95 us -> none  [the longest x8 5.86 us: single_head(): jnp.sum(exponent, axis=-1, keepdims=True)]
    another operation x1 -> x0, local copies, waits for them, and re-layouts: 5.49 us -> none  [heads_attend(): packed.reshape(lines_count, length, 3, HEADS, head_dim)]
  transfers between devices with their start and end apart: 2 -> 0, of which waited for: 2 -> 0; matrix products, arithmetic and copies ran while one was open for 0% -> 0% of each run, Pallas kernels for 0% -> 0%
where the time goes in v1:
time: 139 us; the launch traced here: 138 us
  blocking collectives  118 us (85%)
  Pallas kernels  16.7 us (12%)
  local copies, waits for them, and re-layouts  3.45 us (2%)
    all_to_all x1, blocking collectives, on_device(): lax.all_to_all(to_cols, ('col', 'row'), split_axis=0, concat_axis=0, tile...  49.4 us
    all_to_all x1, blocking collectives, on_device(): cells = lax.all_to_all(grid, 'col', split_axis=0, concat_axis=0, tiled=True)  48.6 us
    all_to_all x1, blocking collectives, on_device(): home = lax.all_to_all(back, 'row', split_axis=0, concat_axis=0, tiled=True)  20.1 us
    pallas_call x2, Pallas kernels, attend(): pl.pallas_call(functools.partial(lines_kernel, lines=lines), out_shape=ja...  16.7 us

profile of v1, /device:TPU:1, one launch (start us, length us, event | category | flops | bytes accessed | tf_op | source)
XLA Modules:
  0.0 138.3 jit_solution(8227232568618560936)
XLA Ops:
  0.0 0.0 copy-start.2
  0.0 0.0 copy-start
  0.0 48.6 %all_to_all.15 = bf16[32,32,256]{2,1,0:T(8,128)(2,1)S(1)} all-to-all(bf16[32,32,256]{2,1,0:T(8,128)(2,1)} %param.7), channel_id=1, replica_groups=mesh['row'=16,'col'=32] {'col'}, dimensions={0} | all-to-all | bytes 1048576 | tf_op jit(solution)/shard_map/all_to_all | solution.py:84
  48.6 0.0 copy-start.4
  48.6 0.0 copy-done.2
  48.6 0.0 copy-done
  48.6 0.7 copy-done.4
  49.3 10.8 %attend_1_lines.1 = bf16[1024,256]{1,0:T(8,128)(2,1)S(1)} custom-call(bf16[1024,256]{1,0:T(8,128)(2,1)S(1)} %bitcast.19, f32[1,256]{1,0:T(1,128)S(1)} %bitcast.20, bf16[256,768]{1,0:T(8,128)(2,1)S(1)} %copy-done, bf16[256,256]{1,0:T(8,128)(2,1)S(1)} %copy-done.2), custom_call_target="tpu_custom_call" | custom-call | tf_op jit(solution)/shard_map/attend_1_lines/pallas_call | solution.py:63
  60.1 0.5 copy.13
  60.6 49.4 %all_to_all.16 = bf16[512,2,256]{2,1,0:T(2,128)(2,1)S(1)} all-to-all(bf16[512,2,256]{2,1,0:T(2,128)(2,1)S(1)} %bitcast.22), channel_id=1, replica_groups=mesh['row'=16,'col'=32] {'col','row'}, dimensions={0} | all-to-all | bytes 1048576 | tf_op jit(solution)/shard_map/all_to_all | solution.py:88
  109.9 0.0 copy-start.1
  110.0 0.0 copy-start.3
  110.0 0.1 copy.14
  110.0 0.0 copy-start.5
  110.0 0.9 copy-done.1
  110.9 0.0 copy-done.3
  111.0 0.0 copy-done.5
  111.0 6.0 %attend_2_lines.1 = bf16[1024,256]{1,0:T(8,128)(2,1)S(1)} custom-call(bf16[1024,256]{1,0:T(8,128)(2,1)S(1)} %bitcast.17, f32[1,256]{1,0:T(1,128)S(1)} %bitcast.21, bf16[256,768]{1,0:T(8,128)(2,1)S(1)} %copy-done.1, bf16[256,256]{1,0:T(8,128)(2,1)S(1)} %copy-done.3), custom_call_target="tpu_custom_call" | custom-call | tf_op jit(solution)/shard_map/attend_2_lines/pallas_call | solution.py:63
  117.0 0.2 copy.18
  117.1 20.1 %all_to_all.17 = bf16[16,32,2,256]{3,1,2,0:T(8,128)(2,1)S(1)} all-to-all(bf16[16,32,2,256]{3,1,2,0:T(8,128)(2,1)S(1)} %bitcast.24), channel_id=1, replica_groups=mesh['row'=16,'col'=32] {'row'}, dimensions={0} | all-to-all | bytes 1048576 | tf_op jit(solution)/shard_map/all_to_all | solution.py:92
  137.2 1.1 copy.16
Async XLA Ops:
  0.0 48.6 %copy-start.2 = (bf16[256,256]{1,0:T(8,128)(2,1)S(1)}, bf16[256,256]{1,0:T(8,128)(2,1)}, u32[]{:S(2)}) copy-start(bf16[256,256]{1,0:T(8,128)(2,1)} %out_ref.2) | copy-start | bytes 393220
  0.0 48.6 %copy-start = (bf16[256,768]{1,0:T(8,128)(2,1)S(1)}, bf16[256,768]{1,0:T(8,128)(2,1)}, u32[]{:S(2)}) copy-start(bf16[256,768]{1,0:T(8,128)(2,1)} %qkv_ref.2) | copy-start | bytes 1179652
  48.6 0.7 copy-start.4
  109.9 1.0 copy-start.1
  110.0 1.0 copy-start.3
  110.0 0.9 copy-start.5

commit v2 on v1

--- a/solution.py
+++ b/solution.py
@@ -6,11 +6,14 @@
 from jax import lax
 from jax.experimental import pallas as pl
 from jax.experimental.pallas import tpu as pltpu
+from jax.sharding import Mesh
 from jax.sharding import PartitionSpec as P
 
 HEADS = 8
+Z_LO = 4
 QUERY_BLOCK = 256
 EPS = 1e-05
+ROW = ("z_lo", "y")
 
 
 def contract(a, b, dim_a, dim_b):
@@ -24,7 +27,19 @@
     return (centred * lax.rsqrt(variance + EPS) * gain).astype(jnp.bfloat16)
 
 
-def lines_kernel(cells_ref, gain_ref, qkv_ref, out_ref, result_ref, q_ref, kt_ref, v_ref, att_ref, *, lines):
+def lines_kernel(*refs, lines, passed):
+    (cells_ref, gain_ref, qkv_ref, out_ref), refs = refs[:4], refs[4:]
+    sources, result_ref, targets = refs[:passed], refs[passed], refs[passed + 1 : 2 * passed + 1]
+    q_ref, kt_ref, v_ref, att_ref, *sems = refs[2 * passed + 1 :]
+    copies = [pltpu.make_async_copy(s, t, sems[0].at[n]) for n, (s, t) in enumerate(zip(sources, targets))]
+    for copy in copies:
+        copy.start()
+    attend_lines(cells_ref, gain_ref, qkv_ref, out_ref, result_ref, q_ref, kt_ref, v_ref, att_ref, lines)
+    for copy in copies:
+        copy.wait()
+
+
+def attend_lines(cells_ref, gain_ref, qkv_ref, out_ref, result_ref, q_ref, kt_ref, v_ref, att_ref, lines):
     cells, width = cells_ref.shape
     length = cells // lines
     head_dim = width // HEADS
@@ -57,45 +72,51 @@
     result_ref[...] = (cells_ref[...].astype(jnp.float32) + added).astype(jnp.bfloat16)
 
 
-def attend(cells, gain, qkv, out, lines):
+def attend(cells, gain, qkv, out, lines, passed=()):
     count, width = cells.shape
-    whole = pl.BlockSpec(memory_space=pltpu.VMEM)
-    return pl.pallas_call(
-        functools.partial(lines_kernel, lines=lines),
-        out_shape=jax.ShapeDtypeStruct((count, width), jnp.bfloat16),
-        in_specs=[whole] * 4,
-        out_specs=whole,
+    whole, anywhere = pl.BlockSpec(memory_space=pltpu.VMEM), pl.BlockSpec(memory_space=pl.ANY)
+    results = pl.pallas_call(
+        functools.partial(lines_kernel, lines=lines, passed=len(passed)),
+        out_shape=[jax.ShapeDtypeStruct(a.shape, a.dtype) for a in (cells, *passed)],
+        in_specs=[whole] * 4 + [anywhere] * len(passed),
+        out_specs=[whole] * (1 + len(passed)),
         scratch_shapes=[
             pltpu.VMEM((count, width), jnp.bfloat16),
             pltpu.VMEM((width, count), jnp.bfloat16),
             pltpu.VMEM((count, width), jnp.bfloat16),
             pltpu.VMEM((count, width), jnp.bfloat16),
-        ],
+        ]
+        + ([pltpu.SemaphoreType.DMA((len(passed),))] if passed else []),
         compiler_params=pltpu.CompilerParams(vmem_limit_bytes=40 << 20),
         name=f"attend_{lines}_lines",
-    )(cells, gain.reshape(1, width), qkv, out)
+    )(cells, gain, qkv, out, *passed)
+    return results if passed else results[0]
 
 
 def on_device(grid, row_gain, row_qkv, row_out, col_gain, col_qkv, col_out):
     rows_blk, cols_blk, width = grid.shape
     col_count = lax.axis_size("col")
-    row_count = lax.axis_size("row")
+    row_count = lax.axis_size(ROW)
     pair = cols_blk // row_count
     cells = lax.all_to_all(grid, "col", split_axis=0, concat_axis=0, tiled=True)
-    middle = attend(cells.reshape(-1, width), row_gain, row_qkv, row_out, 1)
-    to_cols = middle.reshape(col_count, pair, row_count, width).transpose(0, 2, 1, 3)
-    to_cols = to_cols.reshape(col_count * row_count, pair, width)
-    col_cells = lax.all_to_all(to_cols, ("col", "row"), split_axis=0, concat_axis=0, tiled=True)
+    col_weights = (col_gain.reshape(1, width), col_qkv, col_out)
+    middle, *col_weights = attend(
+        cells.reshape(-1, width), row_gain.reshape(1, width), row_qkv, row_out, 1, col_weights
+    )
+    to_cols = middle.reshape(col_count * row_count, pair, width)
+    col_cells = lax.all_to_all(to_cols, ("col", *ROW), split_axis=0, concat_axis=0, tiled=True)
     lines = col_cells.transpose(1, 0, 2).reshape(-1, width)
-    updated = attend(lines, col_gain, col_qkv, col_out, pair)
+    updated = attend(lines, *col_weights, pair)
     back = updated.reshape(pair, col_count, row_count, width).transpose(2, 1, 0, 3)
-    home = lax.all_to_all(back, "row", split_axis=0, concat_axis=0, tiled=True)
-    return home.transpose(1, 2, 0, 3).reshape(rows_blk, cols_blk, width)
+    home = lax.all_to_all(back, ROW, split_axis=0, concat_axis=0, tiled=True)
+    return home.transpose(1, 0, 2, 3).reshape(rows_blk, cols_blk, width)
 
 
 def solution(mesh):
-    in_specs = (P("row", "col", None), P(), P(), P(), P(), P(), P())
-    out_specs = P("row", "col", None)
+    row_count, col_count = mesh.devices.shape
+    split = Mesh(mesh.devices.reshape(row_count // Z_LO, Z_LO, col_count), ("y", "z_lo", "col"))
+    in_specs = (P(("y", "z_lo"), "col", None), P(), P(), P(), P(), P(), P())
+    out_specs = P(("y", "z_lo"), "col", None)
     return jax.shard_map(
-        on_device, mesh=mesh, in_specs=in_specs, out_specs=out_specs, check_vma=False
+        on_device, mesh=split, in_specs=in_specs, out_specs=out_specs, check_vma=False
     )

time: 139 us -> 136 us (0.978)
  blocking collectives: 118 us -> 116 us
    all_to_all x2, blocking collectives: 69.5 us -> 67.6 us  [the longest x1 51.1 us: on_device(): lax.all_to_all(to_cols, ('col', *ROW), split_axis=0, concat_axis=0, tiled...]
where the time goes in v2:
time: 136 us
  blocking collectives  116 us (85%)
  Pallas kernels  17.1 us (13%)
  local copies, waits for them, and re-layouts  2.18 us (2%)
    all_to_all x1, blocking collectives, on_device(): lax.all_to_all(to_cols, ('col', *ROW), split_axis=0, concat_axis=0, tiled...  51.1 us
    all_to_all x1, blocking collectives, on_device(): cells = lax.all_to_all(grid, 'col', split_axis=0, concat_axis=0, tiled=True)  48.6 us
    pallas_call x2, Pallas kernels, attend(): pl.pallas_call(functools.partial(lines_kernel, lines=lines, passed=len(pa...  17.1 us
    all_to_all x1, blocking collectives, on_device(): home = lax.all_to_all(back, ROW, split_axis=0, concat_axis=0, tiled=True)  16.5 us

profile of v2, /device:TPU:1, one launch (start us, length us, event | category | flops | bytes accessed | tf_op | source)
XLA Modules:
  0.0 135.6 jit_solution(14034594017675703950)
XLA Ops:
  0.0 0.0 copy-start.3
  0.0 0.0 copy-start.1
  0.0 0.0 copy-start.2
  0.0 0.0 copy-start
  0.0 0.0 copy-start.5
  0.0 48.6 %all_to_all.15 = bf16[32,32,256]{2,1,0:T(8,128)(2,1)S(1)} all-to-all(bf16[32,32,256]{2,1,0:T(8,128)(2,1)} %param.7), channel_id=1, replica_groups=mesh['y'=4,'z_lo'=4,'col'=32] {'col'}, dimensions={0} | all-to-all | bytes 1048576 | tf_op jit(solution)/shard_map/all_to_all | solution.py:101
  48.7 0.0 copy-start.4
  48.7 0.0 copy-done.3
  48.7 0.0 copy-done.1
  48.7 0.0 copy-done.2
  48.7 0.0 copy-done
  48.7 0.0 copy-done.5
  48.7 0.6 copy-done.4
  49.3 11.1 %attend_1_lines.1 = (bf16[1024,256]{1,0:T(8,128)(2,1)S(1)}, f32[1,256]{1,0:T(1,128)S(1)}, bf16[256,768]{1,0:T(8,128)(2,1)S(1)}, bf16[256,256]{1,0:T(8,128)(2,1)S(1)}) custom-call(bf16[1024,256]{1,0:T(8,128)(2,1)S(1)} %bitcast.12, f32[1,256]{1,0:T(1,128)S(1)} %bitcast.15, bf16[256,768]{1,0:T(8,128)(2,1)S(1)} %copy-done, bf16[256,256]{1,0:T(8,128)(2,1)S(1)} %copy-done.2, ...), custom_call_target="tpu_custom_call" | custom-call | tf_op jit(solution)/shard_map/attend_1_lines/pallas_call | solution.py:78
  60.5 0.2 reshape.24
  60.7 51.1 %all_to_all.16 = bf16[512,2,256]{2,1,0:T(2,128)(2,1)S(1)} all-to-all(bf16[512,2,256]{2,1,0:T(2,128)(2,1)S(1)} %reshape.24), channel_id=1, replica_groups=mesh['y'=4,'z_lo'=4,'col'=32] {'col','z_lo','y'}, dimensions={0} | all-to-all | bytes 1048576 | tf_op jit(solution)/shard_map/all_to_all | solution.py:107
  111.8 0.1 copy.10
  111.9 6.0 %attend_2_lines.1 = bf16[1024,256]{1,0:T(8,128)(2,1)S(1)} custom-call(bf16[1024,256]{1,0:T(8,128)(2,1)S(1)} %bitcast.13, f32[1,256]{1,0:T(1,128)S(1)} %get-tuple-element.10.refs_1_, bf16[256,768]{1,0:T(8,128)(2,1)S(1)} %get-tuple-element.11.refs_2_, bf16[256,256]{1,0:T(8,128)(2,1)S(1)} %get-tuple-element.12.refs_3_), custom_call_target="tpu_custom_call" | custom-call | tf_op jit(solution)/shard_map/attend_2_lines/pallas_call | solution.py:78
  117.9 0.2 copy.14
  118.0 16.5 %all_to_all.17 = bf16[16,32,2,256]{3,1,2,0:T(8,128)(2,1)S(1)} all-to-all(bf16[16,32,2,256]{3,1,2,0:T(8,128)(2,1)S(1)} %bitcast.18), channel_id=1, replica_groups=mesh['y'=4,'z_lo'=4,'col'=32] {'z_lo','y'}, dimensions={0} | all-to-all | bytes 1048576 | tf_op jit(solution)/shard_map/all_to_all | solution.py:111
  134.6 1.1 copy.12
Async XLA Ops:
  0.0 48.7 %copy-start.3 = (bf16[256,256]{1,0:T(8,128)(2,1)S(1)}, bf16[256,256]{1,0:T(8,128)(2,1)}, u32[]{:S(2)}) copy-start(bf16[256,256]{1,0:T(8,128)(2,1)} %refs_6_.1) | copy-start | bytes 393220
  0.0 48.7 %copy-start.1 = (bf16[256,768]{1,0:T(8,128)(2,1)S(1)}, bf16[256,768]{1,0:T(8,128)(2,1)}, u32[]{:S(2)}) copy-start(bf16[256,768]{1,0:T(8,128)(2,1)} %refs_5_.1) | copy-start | bytes 1179652
  0.0 48.7 %copy-start.2 = (bf16[256,256]{1,0:T(8,128)(2,1)S(1)}, bf16[256,256]{1,0:T(8,128)(2,1)}, u32[]{:S(2)}) copy-start(bf16[256,256]{1,0:T(8,128)(2,1)} %refs_3_.1) | copy-start | bytes 393220
  0.0 48.7 %copy-start = (bf16[256,768]{1,0:T(8,128)(2,1)S(1)}, bf16[256,768]{1,0:T(8,128)(2,1)}, u32[]{:S(2)}) copy-start(bf16[256,768]{1,0:T(8,128)(2,1)} %refs_2_.1) | copy-start | bytes 1179652
  0.0 48.7 %copy-start.5 = (f32[256]{0:T(256)S(1)}, f32[256]{0:T(256)}, u32[]{:S(2)}) copy-start(f32[256]{0:T(256)} %param.11) | copy-start | bytes 3076
  48.7 0.7 copy-start.4

commit v3 on v2

--- a/solution.py
+++ b/solution.py
@@ -13,6 +13,7 @@
 Z_LO = 4
 QUERY_BLOCK = 256
 EPS = 1e-05
+ROW_CHUNK = 16
 ROW = ("z_lo", "y")
 
 
@@ -32,14 +33,12 @@
     sources, result_ref, targets = refs[:passed], refs[passed], refs[passed + 1 : 2 * passed + 1]
     q_ref, kt_ref, v_ref, att_ref, *sems = refs[2 * passed + 1 :]
     copies = [pltpu.make_async_copy(s, t, sems[0].at[n]) for n, (s, t) in enumerate(zip(sources, targets))]
-    for copy in copies:
-        copy.start()
-    attend_lines(cells_ref, gain_ref, qkv_ref, out_ref, result_ref, q_ref, kt_ref, v_ref, att_ref, lines)
+    attend_lines(cells_ref, gain_ref, qkv_ref, out_ref, result_ref, q_ref, kt_ref, v_ref, att_ref, lines, copies)
     for copy in copies:
         copy.wait()
 
 
-def attend_lines(cells_ref, gain_ref, qkv_ref, out_ref, result_ref, q_ref, kt_ref, v_ref, att_ref, lines):
+def attend_lines(cells_ref, gain_ref, qkv_ref, out_ref, result_ref, q_ref, kt_ref, v_ref, att_ref, lines, copies):
     cells, width = cells_ref.shape
     length = cells // lines
     head_dim = width // HEADS
@@ -48,6 +47,8 @@
     q_ref[...] = (contract(normed, qkv_ref[:, :width], 1, 0) * scale).astype(jnp.bfloat16)
     kt_ref[...] = contract(qkv_ref[:, width : 2 * width], normed, 0, 1).astype(jnp.bfloat16)
     v_ref[...] = contract(normed, qkv_ref[:, 2 * width :], 1, 0).astype(jnp.bfloat16)
+    for copy in copies:
+        copy.start()
     block = min(QUERY_BLOCK, length)
     head_of_v = lax.broadcasted_iota(jnp.int32, (length, width), 1) // head_dim
     head_of_q = lax.broadcasted_iota(jnp.int32, (block, width), 1) // head_dim
@@ -93,6 +94,27 @@
     return results if passed else results[0]
 
 
+def interleave_kernel(home_ref, grid_ref):
+    places, pair, _, width = home_ref.shape
+    rows = grid_ref.shape[0]
+    start = pl.multiple_of(pl.program_id(0) * rows, rows)
+    lines = home_ref[:, :, pl.ds(start, rows), :].reshape(places * pair, rows, width)
+    grid_ref[...] = jnp.swapaxes(lines, 0, 1)
+
+
+def interleave(home):
+    places, pair, rows, width = home.shape
+    return pl.pallas_call(
+        interleave_kernel,
+        out_shape=jax.ShapeDtypeStruct((rows, places * pair, width), home.dtype),
+        grid=(rows // ROW_CHUNK,),
+        in_specs=[pl.BlockSpec(memory_space=pltpu.VMEM)],
+        out_specs=pl.BlockSpec((ROW_CHUNK, places * pair, width), lambda chunk: (chunk, 0, 0)),
+        compiler_params=pltpu.CompilerParams(vmem_limit_bytes=16 << 20),
+        name="interleave_columns",
+    )(home)
+
+
 def on_device(grid, row_gain, row_qkv, row_out, col_gain, col_qkv, col_out):
     rows_blk, cols_blk, width = grid.shape
     col_count = lax.axis_size("col")
@@ -107,9 +129,9 @@
     col_cells = lax.all_to_all(to_cols, ("col", *ROW), split_axis=0, concat_axis=0, tiled=True)
     lines = col_cells.transpose(1, 0, 2).reshape(-1, width)
     updated = attend(lines, *col_weights, pair)
-    back = updated.reshape(pair, col_count, row_count, width).transpose(2, 1, 0, 3)
+    back = updated.reshape(pair, col_count, row_count, width).transpose(2, 0, 1, 3)
     home = lax.all_to_all(back, ROW, split_axis=0, concat_axis=0, tiled=True)
-    return home.transpose(1, 0, 2, 3).reshape(rows_blk, cols_blk, width)
+    return interleave(home)
 
 
 def solution(mesh):

time: 136 us -> 137 us (level)
  Pallas kernels: 17.1 us -> 18.6 us
where the time goes in v3:
time: 137 us; the launch traced here: 136 us
  blocking collectives  116 us (85%)
  Pallas kernels  18.6 us (14%)
    all_to_all x1, blocking collectives, on_device(): lax.all_to_all(to_cols, ('col', *ROW), split_axis=0, concat_axis=0, tiled...  51.1 us
    all_to_all x1, blocking collectives, on_device(): cells = lax.all_to_all(grid, 'col', split_axis=0, concat_axis=0, tiled=True)  48.6 us
    pallas_call x2, Pallas kernels, attend(): pl.pallas_call(functools.partial(lines_kernel, lines=lines, passed=len(pa...  17.8 us
    all_to_all x1, blocking collectives, on_device(): home = lax.all_to_all(back, ROW, split_axis=0, concat_axis=0, tiled=True)  16.6 us

profile of v3, /device:TPU:1, one launch (start us, length us, event | category | flops | bytes accessed | tf_op | source)
XLA Modules:
  0.0 136.1 jit_solution(13784899882645081128)
XLA Ops:
  0.0 0.0 copy-start.3
  0.0 0.0 copy-start.1
  0.0 0.0 copy-start.2
  0.0 0.0 copy-start
  0.0 0.0 copy-start.5
  0.0 48.6 %all_to_all.15 = bf16[32,32,256]{2,1,0:T(8,128)(2,1)S(1)} all-to-all(bf16[32,32,256]{2,1,0:T(8,128)(2,1)} %param.7), channel_id=1, replica_groups=mesh['y'=4,'z_lo'=4,'col'=32] {'col'}, dimensions={0} | all-to-all | bytes 1048576 | tf_op jit(solution)/shard_map/all_to_all | solution.py:123
  48.7 0.0 copy-start.4
  48.7 0.0 copy-done.3
  48.7 0.0 copy-done.1
  48.7 0.0 copy-done.2
  48.7 0.0 copy-done
  48.7 0.0 copy-done.5
  48.7 0.6 copy-done.4
  49.3 11.8 %attend_1_lines.1 = (bf16[1024,256]{1,0:T(8,128)(2,1)S(1)}, f32[1,256]{1,0:T(1,128)S(1)}, bf16[256,768]{1,0:T(8,128)(2,1)S(1)}, bf16[256,256]{1,0:T(8,128)(2,1)S(1)}) custom-call(bf16[1024,256]{1,0:T(8,128)(2,1)S(1)} %bitcast.9, f32[1,256]{1,0:T(1,128)S(1)} %bitcast.12, bf16[256,768]{1,0:T(8,128)(2,1)S(1)} %copy-done, bf16[256,256]{1,0:T(8,128)(2,1)S(1)} %copy-done.2, ...), custom_call_target="tpu_custom_call" | custom-call | tf_op jit(solution)/shard_map/attend_1_lines/pallas_call | solution.py:79
  61.2 0.2 reshape.21
  61.4 51.1 %all_to_all.16 = bf16[512,2,256]{2,1,0:T(2,128)(2,1)S(1)} all-to-all(bf16[512,2,256]{2,1,0:T(2,128)(2,1)S(1)} %reshape.21), channel_id=1, replica_groups=mesh['y'=4,'z_lo'=4,'col'=32] {'col','z_lo','y'}, dimensions={0} | all-to-all | bytes 1048576 | tf_op jit(solution)/shard_map/all_to_all | solution.py:129
  112.5 0.1 copy.11
  112.5 6.0 %attend_2_lines.1 = bf16[1024,256]{1,0:T(8,128)(2,1)S(1)} custom-call(bf16[1024,256]{1,0:T(8,128)(2,1)S(1)} %bitcast.10, f32[1,256]{1,0:T(1,128)S(1)} %get-tuple-element.10.refs_1_, bf16[256,768]{1,0:T(8,128)(2,1)S(1)} %get-tuple-element.11.refs_2_, bf16[256,256]{1,0:T(8,128)(2,1)S(1)} %get-tuple-element.12.refs_3_), custom_call_target="tpu_custom_call" | custom-call | tf_op jit(solution)/shard_map/attend_2_lines/pallas_call | solution.py:79
  118.5 0.2 copy.14
  118.7 16.6 %all_to_all.17.home_ref = bf16[16,2,32,256]{3,2,1,0:T(8,128)(2,1)S(1)} all-to-all(bf16[16,2,32,256]{3,2,1,0:T(8,128)(2,1)S(1)} %bitcast.15), channel_id=1, replica_groups=mesh['y'=4,'z_lo'=4,'col'=32] {'z_lo','y'}, dimensions={0} | all-to-all | bytes 1048576 | tf_op jit(solution)/shard_map/all_to_all | solution.py:133
  135.2 0.9 interleave_columns.1
Async XLA Ops:
  0.0 48.7 %copy-start.3 = (bf16[256,256]{1,0:T(8,128)(2,1)S(1)}, bf16[256,256]{1,0:T(8,128)(2,1)}, u32[]{:S(2)}) copy-start(bf16[256,256]{1,0:T(8,128)(2,1)} %refs_6_.1) | copy-start | bytes 393220
  0.0 48.7 %copy-start.1 = (bf16[256,768]{1,0:T(8,128)(2,1)S(1)}, bf16[256,768]{1,0:T(8,128)(2,1)}, u32[]{:S(2)}) copy-start(bf16[256,768]{1,0:T(8,128)(2,1)} %refs_5_.1) | copy-start | bytes 1179652
  0.0 48.7 %copy-start.2 = (bf16[256,256]{1,0:T(8,128)(2,1)S(1)}, bf16[256,256]{1,0:T(8,128)(2,1)}, u32[]{:S(2)}) copy-start(bf16[256,256]{1,0:T(8,128)(2,1)} %refs_3_.1) | copy-start | bytes 393220
  0.0 48.7 %copy-start = (bf16[256,768]{1,0:T(8,128)(2,1)S(1)}, bf16[256,768]{1,0:T(8,128)(2,1)}, u32[]{:S(2)}) copy-start(bf16[256,768]{1,0:T(8,128)(2,1)} %refs_2_.1) | copy-start | bytes 1179652
  0.0 48.7 %copy-start.5 = (f32[256]{0:T(256)S(1)}, f32[256]{0:T(256)}, u32[]{:S(2)}) copy-start(f32[256]{0:T(256)} %param.11) | copy-start | bytes 3076
  48.7 0.7 copy-start.4

commit v4 on v3

--- a/solution.py
+++ b/solution.py
@@ -10,10 +10,13 @@
 from jax.sharding import PartitionSpec as P
 
 HEADS = 8
+Z_HI = 4
+CORES = 2
 Z_LO = 4
 QUERY_BLOCK = 256
 EPS = 1e-05
 ROW_CHUNK = 16
+COL = ("z_hi", "core", "x")
 ROW = ("z_lo", "y")
 
 
@@ -33,12 +36,14 @@
     sources, result_ref, targets = refs[:passed], refs[passed], refs[passed + 1 : 2 * passed + 1]
     q_ref, kt_ref, v_ref, att_ref, *sems = refs[2 * passed + 1 :]
     copies = [pltpu.make_async_copy(s, t, sems[0].at[n]) for n, (s, t) in enumerate(zip(sources, targets))]
-    attend_lines(cells_ref, gain_ref, qkv_ref, out_ref, result_ref, q_ref, kt_ref, v_ref, att_ref, lines, copies)
+    for copy in copies:
+        copy.start()
+    attend_lines(cells_ref, gain_ref, qkv_ref, out_ref, result_ref, q_ref, kt_ref, v_ref, att_ref, lines)
     for copy in copies:
         copy.wait()
 
 
-def attend_lines(cells_ref, gain_ref, qkv_ref, out_ref, result_ref, q_ref, kt_ref, v_ref, att_ref, lines, copies):
+def attend_lines(cells_ref, gain_ref, qkv_ref, out_ref, result_ref, q_ref, kt_ref, v_ref, att_ref, lines):
     cells, width = cells_ref.shape
     length = cells // lines
     head_dim = width // HEADS
@@ -47,8 +52,6 @@
     q_ref[...] = (contract(normed, qkv_ref[:, :width], 1, 0) * scale).astype(jnp.bfloat16)
     kt_ref[...] = contract(qkv_ref[:, width : 2 * width], normed, 0, 1).astype(jnp.bfloat16)
     v_ref[...] = contract(normed, qkv_ref[:, 2 * width :], 1, 0).astype(jnp.bfloat16)
-    for copy in copies:
-        copy.start()
     block = min(QUERY_BLOCK, length)
     head_of_v = lax.broadcasted_iota(jnp.int32, (length, width), 1) // head_dim
     head_of_q = lax.broadcasted_iota(jnp.int32, (block, width), 1) // head_dim
@@ -117,16 +120,16 @@
 
 def on_device(grid, row_gain, row_qkv, row_out, col_gain, col_qkv, col_out):
     rows_blk, cols_blk, width = grid.shape
-    col_count = lax.axis_size("col")
+    col_count = lax.axis_size(COL)
     row_count = lax.axis_size(ROW)
     pair = cols_blk // row_count
-    cells = lax.all_to_all(grid, "col", split_axis=0, concat_axis=0, tiled=True)
+    cells = lax.all_to_all(grid, COL, split_axis=0, concat_axis=0, tiled=True)
     col_weights = (col_gain.reshape(1, width), col_qkv, col_out)
     middle, *col_weights = attend(
         cells.reshape(-1, width), row_gain.reshape(1, width), row_qkv, row_out, 1, col_weights
     )
     to_cols = middle.reshape(col_count * row_count, pair, width)
-    col_cells = lax.all_to_all(to_cols, ("col", *ROW), split_axis=0, concat_axis=0, tiled=True)
+    col_cells = lax.all_to_all(to_cols, (*COL, *ROW), split_axis=0, concat_axis=0, tiled=True)
     lines = col_cells.transpose(1, 0, 2).reshape(-1, width)
     updated = attend(lines, *col_weights, pair)
     back = updated.reshape(pair, col_count, row_count, width).transpose(2, 0, 1, 3)
@@ -135,10 +138,10 @@
 
 
 def solution(mesh):
-    row_count, col_count = mesh.devices.shape
-    split = Mesh(mesh.devices.reshape(row_count // Z_LO, Z_LO, col_count), ("y", "z_lo", "col"))
-    in_specs = (P(("y", "z_lo"), "col", None), P(), P(), P(), P(), P(), P())
-    out_specs = P(("y", "z_lo"), "col", None)
+    row_count, _ = mesh.devices.shape
+    split = Mesh(mesh.devices.reshape(row_count // Z_LO, Z_LO, Z_HI, -1, CORES), ("y", "z_lo", "z_hi", "x", "core"))
+    in_specs = (P(("y", "z_lo"), ("z_hi", "x", "core"), None), P(), P(), P(), P(), P(), P())
+    out_specs = P(("y", "z_lo"), ("z_hi", "x", "core"), None)
     return jax.shard_map(
         on_device, mesh=split, in_specs=in_specs, out_specs=out_specs, check_vma=False
     )

time: 137 us -> 136 us (level)
  no operation moved by 1% of the time
where the time goes in v4:
time: 136 us; the launch traced here: 135 us
  blocking collectives  116 us (85%)
  Pallas kernels  18 us (13%)
    all_to_all x1, blocking collectives, on_device(): lax.all_to_all(to_cols, (*COL, *ROW), split_axis=0, concat_axis=0, tiled=...  50.6 us
    all_to_all x1, blocking collectives, on_device(): cells = lax.all_to_all(grid, COL, split_axis=0, concat_axis=0, tiled=True)  48.7 us
    pallas_call x2, Pallas kernels, attend(): pl.pallas_call(functools.partial(lines_kernel, lines=lines, passed=len(pa...  17.1 us
    all_to_all x1, blocking collectives, on_device(): home = lax.all_to_all(back, ROW, split_axis=0, concat_axis=0, tiled=True)  16.6 us

profile of v4, /device:TPU:1, one launch (start us, length us, event | category | flops | bytes accessed | tf_op | source)
XLA Modules:
  0.0 135.1 jit_solution(8695155329888402001)
XLA Ops:
  0.0 0.0 copy-start.3
  0.0 0.0 copy-start.1
  0.0 0.0 copy-start.2
  0.0 0.0 copy-start
  0.0 0.0 copy-start.5
  0.0 48.7 %all_to_all.15 = bf16[32,32,256]{2,1,0:T(8,128)(2,1)S(1)} all-to-all(bf16[32,32,256]{2,1,0:T(8,128)(2,1)} %param.7), channel_id=1, replica_groups=mesh['y'=4,'z_lo'=4,'z_hi'=4,'x'=4,'core'=2] {'z_hi','core','x'}, dimensions={0} | all-to-all | bytes 1048576 | tf_op jit(solution)/shard_map/all_to_all | solution.py:126
  48.7 0.0 copy-start.4
  48.7 0.0 copy-done.3
  48.7 0.0 copy-done.1
  48.7 0.0 copy-done.2
  48.7 0.0 copy-done
  48.7 0.0 copy-done.5
  48.8 0.6 copy-done.4
  49.4 11.1 %attend_1_lines.1 = (bf16[1024,256]{1,0:T(8,128)(2,1)S(1)}, f32[1,256]{1,0:T(1,128)S(1)}, bf16[256,768]{1,0:T(8,128)(2,1)S(1)}, bf16[256,256]{1,0:T(8,128)(2,1)S(1)}) custom-call(bf16[1024,256]{1,0:T(8,128)(2,1)S(1)} %bitcast.9, f32[1,256]{1,0:T(1,128)S(1)} %bitcast.12, bf16[256,768]{1,0:T(8,128)(2,1)S(1)} %copy-done, bf16[256,256]{1,0:T(8,128)(2,1)S(1)} %copy-done.2, ...), custom_call_target="tpu_custom_call" | custom-call | tf_op jit(solution)/shard_map/attend_1_lines/pallas_call | solution.py:82
  60.6 0.2 reshape.21
  60.8 50.6 %all_to_all.16 = bf16[512,2,256]{2,1,0:T(2,128)(2,1)S(1)} all-to-all(bf16[512,2,256]{2,1,0:T(2,128)(2,1)S(1)} %reshape.21), channel_id=1, replica_groups=mesh['y'=4,'z_lo'=4,'z_hi'=4,'x'=4,'core'=2] {'z_hi','core','x','z_lo','y'}, dimensions={0} | all-to-all | bytes 1048576 | tf_op jit(solution)/shard_map/all_to_all | solution.py:132
  111.3 0.1 copy.11
  111.4 6.0 %attend_2_lines.1 = bf16[1024,256]{1,0:T(8,128)(2,1)S(1)} custom-call(bf16[1024,256]{1,0:T(8,128)(2,1)S(1)} %bitcast.10, f32[1,256]{1,0:T(1,128)S(1)} %get-tuple-element.10.refs_1_, bf16[256,768]{1,0:T(8,128)(2,1)S(1)} %get-tuple-element.11.refs_2_, bf16[256,256]{1,0:T(8,128)(2,1)S(1)} %get-tuple-element.12.refs_3_), custom_call_target="tpu_custom_call" | custom-call | tf_op jit(solution)/shard_map/attend_2_lines/pallas_call | solution.py:82
  117.4 0.2 copy.14
  117.6 16.6 %all_to_all.17.home_ref = bf16[16,2,32,256]{3,2,1,0:T(8,128)(2,1)S(1)} all-to-all(bf16[16,2,32,256]{3,2,1,0:T(8,128)(2,1)S(1)} %bitcast.15), channel_id=1, replica_groups=mesh['y'=4,'z_lo'=4,'z_hi'=4,'x'=4,'core'=2] {'z_lo','y'}, dimensions={0} | all-to-all | bytes 1048576 | tf_op jit(solution)/shard_map/all_to_all | solution.py:136
  134.2 0.9 interleave_columns.1
Async XLA Ops:
  0.0 48.7 %copy-start.3 = (bf16[256,256]{1,0:T(8,128)(2,1)S(1)}, bf16[256,256]{1,0:T(8,128)(2,1)}, u32[]{:S(2)}) copy-start(bf16[256,256]{1,0:T(8,128)(2,1)} %refs_6_.1) | copy-start | bytes 393220
  0.0 48.7 %copy-start.1 = (bf16[256,768]{1,0:T(8,128)(2,1)S(1)}, bf16[256,768]{1,0:T(8,128)(2,1)}, u32[]{:S(2)}) copy-start(bf16[256,768]{1,0:T(8,128)(2,1)} %refs_5_.1) | copy-start | bytes 1179652
  0.0 48.7 %copy-start.2 = (bf16[256,256]{1,0:T(8,128)(2,1)S(1)}, bf16[256,256]{1,0:T(8,128)(2,1)}, u32[]{:S(2)}) copy-start(bf16[256,256]{1,0:T(8,128)(2,1)} %refs_3_.1) | copy-start | bytes 393220
  0.0 48.7 %copy-start = (bf16[256,768]{1,0:T(8,128)(2,1)S(1)}, bf16[256,768]{1,0:T(8,128)(2,1)}, u32[]{:S(2)}) copy-start(bf16[256,768]{1,0:T(8,128)(2,1)} %refs_2_.1) | copy-start | bytes 1179652
  0.0 48.7 %copy-start.5 = (f32[256]{0:T(256)S(1)}, f32[256]{0:T(256)}, u32[]{:S(2)}) copy-start(f32[256]{0:T(256)} %param.11) | copy-start | bytes 3076
  48.7 0.7 copy-start.4
